TPU v7x, 32 devices: a whole 2x2x4 slice. The times are simulated.
32 devices in a mesh: gx: 4 (over z), gy: 4 (over y, x), gz: 2 (over core).
Axes of the slice: x: 2, y: 2, z: 4, core: 2. Of those that a mesh axis runs over, the one named last changes fastest.
Arguments:
- adj_e: float32 [2, 3, 32, 64, 512], P(None, None, 'gy', 'gz', 'gx'), may hold values from -6 to 6
- adj_h: float32 [2, 3, 32, 64, 512], P(None, None, 'gy', 'gz', 'gx'), may hold values from -6 to 6
- fwd_e: bfloat16 [2, 2, 3, 32, 64, 512], P(None, None, None, 'gy', 'gz', 'gx'), may hold values from -6 to 6
- material: int32 [32, 64, 512], P('gy', 'gz', 'gx'), may hold values from 0 to 3
- eps_table: float32 [4], replicated, may hold values from 0.6 to 1
Outputs:
- new_e: float32 [2, 3, 32, 64, 512], P(None, None, 'gy', 'gz', 'gx')
- new_h: float32 [2, 3, 32, 64, 512], P(None, None, 'gy', 'gz', 'gx')
- grad_eps: float32 [32, 64, 512], P('gy', 'gz', 'gx')
Inputs may be any that keep to these rules, and one draw needn't show every extreme that they name: `material`: a valid index into eps_table.
All inputs are finite; a program needn't handle non-finite values.
Results may differ from a plain program's by a relative error of at most 0.0003.
Values sent between devices are 32-bit elements; how exact they have to be, the bound alone decides.
A program may use at most 128 MiB of HBM per device.

v0:
```python
import math

import jax
import jax.numpy as jnp
from jax import lax
from jax.sharding import PartitionSpec as P

time_step = 0.4
cosine_x = math.cos(1.3)
sine_x = math.sin(1.3)
cosine_y = math.cos(0.7)
sine_y = math.sin(0.7)


def passed_along(shard, axis, by):
    length = lax.axis_size(axis)
    return lax.ppermute(shard, axis, [(i, (i + by) % length) for i in range(length)])


def passed_along_2(block, axis, distance):
    devices = range(lax.axis_size(axis))
    route = [(i - distance, i) for i in devices if i - distance in devices]
    return lax.ppermute(block, axis, route)


def rotate_pair(pair, cosine, sine):
    return jnp.stack([pair[0] * cosine - pair[1] * sine, pair[0] * sine + pair[1] * cosine])


def neighbour_prior(field, rim, axis):
    extent = field.shape[axis]
    inner = lax.slice_in_dim(field, 0, extent - 1, axis=axis)
    return jnp.concatenate([jnp.expand_dims(rim, axis), inner], axis=axis)


def neighbour_later(field, rim, axis):
    extent = field.shape[axis]
    inner = lax.slice_in_dim(field, 1, extent, axis=axis)
    return jnp.concatenate([inner, jnp.expand_dims(rim, axis)], axis=axis)


def update_faces(e_field, h_field, inverse_eps):
    place_x = lax.axis_index("gx")
    count_x = lax.axis_size("gx")
    place_y = lax.axis_index("gy")
    count_y = lax.axis_size("gy")
    rim_x = passed_along(h_field[:, 1:3, :, :, -1], "gx", 1)
    rim_x = jnp.where(place_x == 0, rotate_pair(rim_x, cosine_x, -sine_x), rim_x)
    rim_y = passed_along(h_field[:, 0::2, -1], "gy", 1)
    rim_y = jnp.where(place_y == 0, rotate_pair(rim_y, cosine_y, -sine_y), rim_y)
    rim_z = passed_along_2(h_field[:, 0:2, :, -1], "gz", 1)
    h_xcomp, h_ycomp, h_zcomp = (h_field[:, 0], h_field[:, 1], h_field[:, 2])
    curl_x = (
        h_zcomp
        - neighbour_prior(h_zcomp, rim_y[:, 1], 1)
        - (h_ycomp - neighbour_prior(h_ycomp, rim_z[:, 1], 2))
    )
    curl_y = (
        h_xcomp
        - neighbour_prior(h_xcomp, rim_z[:, 0], 2)
        - (h_zcomp - neighbour_prior(h_zcomp, rim_x[:, 1], 3))
    )
    curl_z = (
        h_ycomp
        - neighbour_prior(h_ycomp, rim_x[:, 0], 3)
        - (h_xcomp - neighbour_prior(h_xcomp, rim_y[:, 0], 1))
    )
    e_field = e_field - time_step * inverse_eps * jnp.stack([curl_x, curl_y, curl_z], 1)
    lead_x = passed_along(e_field[:, 1:3, :, :, 0], "gx", -1)
    lead_x = jnp.where(place_x == count_x - 1, rotate_pair(lead_x, cosine_x, sine_x), lead_x)
    lead_y = passed_along(e_field[:, 0::2, 0], "gy", -1)
    lead_y = jnp.where(place_y == count_y - 1, rotate_pair(lead_y, cosine_y, sine_y), lead_y)
    lead_z = passed_along_2(e_field[:, 0:2, :, 0], "gz", -1)
    e_xcomp, e_ycomp, e_zcomp = (e_field[:, 0], e_field[:, 1], e_field[:, 2])
    rise_x = (
        neighbour_later(e_zcomp, lead_y[:, 1], 1)
        - e_zcomp
        - (neighbour_later(e_ycomp, lead_z[:, 1], 2) - e_ycomp)
    )
    rise_y = (
        neighbour_later(e_xcomp, lead_z[:, 0], 2)
        - e_xcomp
        - (neighbour_later(e_zcomp, lead_x[:, 1], 3) - e_zcomp)
    )
    rise_z = (
        neighbour_later(e_ycomp, lead_x[:, 0], 3)
        - e_ycomp
        - (neighbour_later(e_xcomp, lead_y[:, 0], 1) - e_xcomp)
    )
    h_field = h_field + time_step * jnp.stack([rise_x, rise_y, rise_z], 1)
    return (e_field, h_field)


def shards(adj_e, adj_h, fwd_e, material, eps_table):
    inverse_eps = jnp.zeros(material.shape, jnp.float32)
    for which in range(eps_table.shape[0]):
        inverse_eps = jnp.where(material == which, 1.0 / eps_table[which], inverse_eps)
    e_field = adj_e
    h_field = adj_h
    grad_eps = jnp.zeros(material.shape, jnp.float32)
    sections = fwd_e.shape[0]
    for section in range(sections):
        e_field, h_next = update_faces(e_field, h_field, inverse_eps)
        grad_eps = grad_eps + inverse_eps * jnp.sum(
            e_field * fwd_e[section].astype(jnp.float32), axis=(0, 1)
        )
        h_field = h_next
    return (e_field, h_field, grad_eps)


def solution(mesh):
    return jax.shard_map(
        shards,
        mesh=mesh,
        in_specs=(
            P(None, None, "gy", "gz", "gx"),
            P(None, None, "gy", "gz", "gx"),
            P(None, None, None, "gy", "gz", "gx"),
            P("gy", "gz", "gx"),
            P(),
        ),
        out_specs=(
            P(None, None, "gy", "gz", "gx"),
            P(None, None, "gy", "gz", "gx"),
            P("gy", "gz", "gx"),
        ),
        check_vma=False,
    )
```

profile of v0, /device:TPU:0, one launch (start us, length us, event | category | flops | bytes accessed | tf_op | source)
XLA Modules:
  0.0 80.6 jit_solution(16875834845349845828)
XLA Ops:
  0.6 1.3 %slice.315 = f32[2,2,8,32,1]{4,3,2,1,0:T(8,128)S(1)} slice(f32[2,3,8,32,128]{4,3,2,1,0:T(8,128)} %param.6), slice={[0:2], [1:3], [0:8], [0:32], [127:128]} | slice | bytes 8192 | tf_op jit(solution)/shard_map/slice | solution.py:47
  2.8 3.0 %collective-permute-start.2 = (f32[2,2,8,32]{3,2,0,1:T(8,128)}, f32[2,2,8,32]{3,2,0,1:T(8,128)S(1)}, u32[]{:S(2)}, u32[]{:S(2)}) collective-permute-start(f32[2,2,8,32]{3,2,0,1:T(8,128)} %bitcast.22), channel_id=1, source_target_pairs={{0,8},{8,16},{16,24},{24,0},{1,9},{9,17},{17,25},{25,1},{2,10},{10... | collective-permute-start | bytes 12296 | tf_op jit(solution)/shard_map/ppermute | solution.py:17
  5.9 1.5 %collective-permute-start = (f32[2,2,32,128]{3,2,0,1:T(8,128)S(1)}, f32[2,2,32,128]{3,2,0,1:T(8,128)S(1)}, u32[]{:S(2)}, u32[]{:S(2)}) collective-permute-start(f32[2,2,32,128]{3,2,0,1:T(8,128)S(1)} %copy_bitcast_fusion.3), channel_id=1, source_target_pairs={{0,2},{2,4},{4,6},{6,0},{1,3},{3,5},{5,7},{7,1},{8,10},{10,12},{12... | collective-permute-start | bytes 196616 | tf_op jit(solution)/shard_map/ppermute | solution.py:17
  8.0 1.9 %collective-permute-start.1 = (f32[2,2,8,128]{3,2,0,1:T(8,128)}, f32[2,2,8,128]{3,2,0,1:T(8,128)}, u32[]{:S(2)}, u32[]{:S(2)}) collective-permute-start(f32[2,2,8,128]{3,2,0,1:T(8,128)} %bitcast.262), channel_id=1, source_target_pairs={{0,1},{2,3},{4,5},{6,7},{8,9},{10,11},{12,13},{14,15},{16,17},{18,... | collective-permute-start | bytes 49160 | tf_op jit(solution)/shard_map/ppermute | solution.py:23
  14.4 2.0 %fusion.32 = (bf16[1,2,3,8,32,128]{5,4,3,2,1,0:T(8,128)(2,1)S(1)}, bf16[1,2,3,8,32,128]{5,4,3,2,1,0:T(8,128)(2,1)}) fusion(bf16[2,2,3,8,32,128]{5,4,3,2,1,0:T(8,128)(2,1)} %param.7), kind=kLoop, calls=%fused_computation.161 | loop fusion | bytes 1572864 | tf_op jit(solution)/shard_map/slice | solution.py:105
  19.7 1.3 %fusion.6 = (f32[2,1,8,32,128]{4,3,2,1,0:T(8,128)S(1)}, f32[2,1,8,32,128]{4,3,2,1,0:T(8,128)S(1)}, f32[2,1,8,32,128]{4,3,2,1,0:T(8,128)S(1)}) fusion(f32[2,1,7,32,128]{4,3,2,1,0:T(8,128)} %get-tuple-element.135, f32[2,1,1,32,128]{4,3,2,1,0:T(8,128)S(1)} %get-tuple-element.98, f32[2,1,8,31,128]{4,3,2,1,0:T(8,128)S(1)} %copy-done.11, ...), kind=kLoop, calls=%fused_computation.35 | loop fusion | flops 983040 | bytes 3145728 | tf_op jit(solution)/shard_map/sub | solution.py:54
  24.8 2.3 %collective-permute-start.5 = (f32[2,2,8,32]{3,2,0,1:T(8,128)S(1)}, f32[2,2,8,32]{3,2,0,1:T(8,128)S(1)}, u32[]{:S(2)}, u32[]{:S(2)}) collective-permute-start(f32[2,2,8,32]{3,2,0,1:T(8,128)S(1)} %bitcast.269), channel_id=1, source_target_pairs={{0,24},{8,0},{16,8},{24,16},{1,25},{9,1},{17,9},{25,17},{2,26},{10... | collective-permute-start | bytes 12296 | tf_op jit(solution)/shard_map/ppermute | solution.py:17
  27.1 1.4 %collective-permute-start.3 = (f32[2,2,32,128]{3,2,1,0:T(8,128)S(1)}, f32[2,2,32,128]{3,2,1,0:T(8,128)S(1)}, u32[]{:S(2)}, u32[]{:S(2)}) collective-permute-start(f32[2,2,32,128]{3,2,1,0:T(8,128)S(1)} %slice_bitcast_fusion.37), channel_id=1, source_target_pairs={{0,6},{2,0},{4,2},{6,4},{1,7},{3,1},{5,3},{7,5},{8,14},{10,8},{12,... | collective-permute-start | bytes 196616 | tf_op jit(solution)/shard_map/ppermute | solution.py:17
  28.6 1.3 %collective-permute-start.4 = (f32[2,2,8,128]{3,2,1,0:T(8,128)S(1)}, f32[2,2,8,128]{3,2,1,0:T(8,128)S(1)}, u32[]{:S(2)}, u32[]{:S(2)}) collective-permute-start(f32[2,2,8,128]{3,2,1,0:T(8,128)S(1)} %bitcast.271), channel_id=1, source_target_pairs={{1,0},{3,2},{5,4},{7,6},{9,8},{11,10},{13,12},{15,14},{17,16},{19,... | collective-permute-start | bytes 49160 | tf_op jit(solution)/shard_map/ppermute | solution.py:23
  29.9 1.0 %copy.1373 = f32[8,32,128]{1,0,2:T(8,128)} copy(f32[8,32,128]{2,1,0:T(8,128)S(1)} %copy-done.21) | data formatting | bytes 262144
  33.7 1.5 %fusion.9 = (f32[2,1,8,32,128]{4,3,1,0,2:T(8,128)S(1)}, f32[2,1,8,32,128]{4,3,1,0,2:T(8,128)S(1)}, f32[2,1,8,32,128]{4,3,1,0,2:T(8,128)S(1)}) fusion(f32[2,1,1,32,128]{4,3,1,0,2:T(8,128)S(1)} %get-tuple-element.94, f32[2,1,7,32,128]{4,3,1,0,2:T(8,128)} %slice_bitcast_fusion.33, f32[2,1,8,1,128]{4,3,0,2,1:T(1,128)S(1)} %copy.1320, ...), kind=kLoop, calls=%fused_computation.44 | loop fusion | flops 983040 | bytes 3145728 | tf_op jit(solution)/shard_map/sub | solution.py:76
  36.0 1.0 %slice.441 = f32[2,2,8,32,1]{4,3,1,0,2:T(8,128)} slice(f32[2,3,8,32,128]{4,3,1,0,2:T(8,128)S(1)} %fusion), slice={[0:2], [1:3], [0:8], [0:32], [127:128]} | slice | bytes 8192 | tf_op jit(solution)/shard_map/slice | solution.py:47
  41.3 1.3 %copy.1371 = f32[2,2,8,32,1]{3,2,0,1,4:T(8,128)S(1)} copy(f32[2,2,8,32,1]{4,3,1,0,2:T(8,128)} %slice.441) | data formatting | bytes 8192 | tf_op jit(solution)/shard_map/squeeze | solution.py:47
  44.7 3.2 %collective-permute-start.7 = (f32[2,2,8,128]{3,2,1,0:T(8,128)}, f32[2,2,8,128]{3,2,1,0:T(8,128)}, u32[]{:S(2)}, u32[]{:S(2)}) collective-permute-start(f32[2,2,8,128]{3,2,1,0:T(8,128)} %bitcast.264), channel_id=1, source_target_pairs={{0,1},{2,3},{4,5},{6,7},{8,9},{10,11},{12,13},{14,15},{16,17},{18,... | collective-permute-start | bytes 49160 | tf_op jit(solution)/shard_map/ppermute | solution.py:23
  51.7 1.2 %fusion.16 = f32[2,1,8,32,128]{4,3,1,0,2:T(8,128)S(1)} fusion(f32[2,1,7,32,128]{4,3,0,2,1:T(8,128)} %slice_bitcast_fusion.31, f32[2,1,1,32,128]{4,3,0,2,1:T(8,128)S(1)} %get-tuple-element.90, f32[2,1,8,31,128]{4,3,0,2,1:T(8,128)S(1)} %copy-done.12, f32[2,1,8,1,128]{4,3,0,2,1:T(1,128)S(1)} %copy.1339, f32[2,3,8,32,128]{4,3,1,0,2:T(8,128)S(1)} %fusion), kind=kLoop, calls=%fused_computation.57 | loop fusion | flops 327680 | bytes 1310720 | tf_op jit(solution)/shard_map/sub | solution.py:54
  60.7 1.0 %copy.1374 = f32[8,32,128]{1,0,2:T(8,128)} copy(f32[8,32,128]{2,1,0:T(8,128)S(1)} %copy-done.22) | data formatting | bytes 262144
  61.7 1.3 %copy.1372 = f32[2,2,8,32,1]{3,2,0,1,4:T(8,128)S(1)} copy(f32[2,2,8,32,1]{4,3,1,0,2:T(8,128)} %slice.463) | data formatting | bytes 8192 | tf_op jit(solution)/shard_map/squeeze | solution.py:69
  63.0 3.3 %collective-permute-start.11 = (f32[2,2,8,32]{3,2,0,1:T(8,128)S(1)}, f32[2,2,8,32]{3,2,0,1:T(8,128)S(1)}, u32[]{:S(2)}, u32[]{:S(2)}) collective-permute-start(f32[2,2,8,32]{3,2,0,1:T(8,128)S(1)} %bitcast.268), channel_id=1, source_target_pairs={{0,24},{8,0},{16,8},{24,16},{1,25},{9,1},{17,9},{25,17},{2,26},{10... | collective-permute-start | bytes 12296 | tf_op jit(solution)/shard_map/ppermute | solution.py:17
  66.3 2.0 %add_multiply_fusion = f32[8,32,128]{1,0,2:T(8,128)} fusion(f32[8,32,128]{1,0,2:T(8,128)S(1)} %copy-done.3, f32[8,32,128]{1,0,2:T(8,128)} %copy.1374, s32[8,32,128]{1,0,2:T(8,128)S(1)} %copy.1293, f32[]{:T(128)} %bitcast.3, f32[]{:T(128)} %bitcast.2, f32[]{:T(128)} %bitcast.1, f32[]{:T(128)} %bitcast), kind=kLoop, calls=%fused_computation.13 | loop fusion | flops 327680 | bytes 524304 | tf_op jit(solution)/shard_map/add | solution.py:104
  68.4 0.9 %copy.1367 = f32[2,3,8,32,128]{4,3,2,1,0:T(8,128)} copy(f32[2,3,8,32,128]{4,3,1,0,2:T(8,128)S(1)} %get-tuple-element.58) | data formatting | bytes 1572864
  70.4 3.1 %collective-permute-start.9 = (f32[2,2,32,128]{3,2,1,0:T(8,128)S(1)}, f32[2,2,32,128]{3,2,1,0:T(8,128)S(1)}, u32[]{:S(2)}, u32[]{:S(2)}) collective-permute-start(f32[2,2,32,128]{3,2,1,0:T(8,128)S(1)} %slice_bitcast_fusion.36), channel_id=1, source_target_pairs={{0,6},{2,0},{4,2},{6,4},{1,7},{3,1},{5,3},{7,5},{8,14},{10,8},{12,... | collective-permute-start | bytes 196616 | tf_op jit(solution)/shard_map/ppermute | solution.py:17
  73.5 1.3 %collective-permute-start.10 = (f32[2,2,8,128]{3,2,1,0:T(8,128)S(1)}, f32[2,2,8,128]{3,2,1,0:T(8,128)S(1)}, u32[]{:S(2)}, u32[]{:S(2)}) collective-permute-start(f32[2,2,8,128]{3,2,1,0:T(8,128)S(1)} %bitcast.272), channel_id=1, source_target_pairs={{1,0},{3,2},{5,4},{7,6},{9,8},{11,10},{13,12},{15,14},{17,16},{19,... | collective-permute-start | bytes 49160 | tf_op jit(solution)/shard_map/ppermute | solution.py:23
  77.7 1.7 %fusion.21 = (f32[2,1,8,32,128]{4,3,1,0,2:T(8,128)S(1)}, f32[2,1,8,32,128]{4,3,1,0,2:T(8,128)S(1)}, f32[2,1,8,32,128]{4,3,1,0,2:T(8,128)S(1)}) fusion(f32[2,1,1,32,128]{4,3,1,0,2:T(8,128)S(1)} %get-tuple-element.86, f32[2,1,7,32,128]{4,3,1,0,2:T(8,128)} %slice_bitcast_fusion.29, f32[2,1,8,1,128]{4,3,0,2,1:T(1,128)S(1)} %copy.1353, ...), kind=kLoop, calls=%fused_computation.68 | loop fusion | flops 983040 | bytes 3145728 | tf_op jit(solution)/shard_map/sub | solution.py:76
  79.7 0.9 %copy.1368 = f32[2,3,8,32,128]{4,3,2,1,0:T(8,128)} copy(f32[2,3,8,32,128]{4,3,1,0,2:T(8,128)S(1)} %fusion.2) | data formatting | bytes 1572864
  (157 shorter events, 35.9 us)
Async XLA Ops:
  0.6 5.2 %copy-start = (f32[2,3,8,32,128]{4,3,2,1,0:T(8,128)S(1)}, f32[2,3,8,32,128]{4,3,2,1,0:T(8,128)}, u32[]{:S(2)}) copy-start(f32[2,3,8,32,128]{4,3,2,1,0:T(8,128)} %param.6) | copy-start | bytes 2359300
  2.8 14.7 %collective-permute-start.2 = (f32[2,2,8,32]{3,2,0,1:T(8,128)}, f32[2,2,8,32]{3,2,0,1:T(8,128)S(1)}, u32[]{:S(2)}, u32[]{:S(2)}) collective-permute-start(f32[2,2,8,32]{3,2,0,1:T(8,128)} %bitcast.22), channel_id=1, source_target_pairs={{0,8},{8,16},{16,24},{24,0},{1,9},{9,17},{17,25},{25,1},{2,10},{10... | collective-permute-start | bytes 12296 | tf_op jit(solution)/shard_map/ppermute | solution.py:17
  5.9 12.9 %collective-permute-start = (f32[2,2,32,128]{3,2,0,1:T(8,128)S(1)}, f32[2,2,32,128]{3,2,0,1:T(8,128)S(1)}, u32[]{:S(2)}, u32[]{:S(2)}) collective-permute-start(f32[2,2,32,128]{3,2,0,1:T(8,128)S(1)} %copy_bitcast_fusion.3), channel_id=1, source_target_pairs={{0,2},{2,4},{4,6},{6,0},{1,3},{3,5},{5,7},{7,1},{8,10},{10,12},{12... | collective-permute-start | bytes 196616 | tf_op jit(solution)/shard_map/ppermute | solution.py:17
  8.0 9.9 %collective-permute-start.1 = (f32[2,2,8,128]{3,2,0,1:T(8,128)}, f32[2,2,8,128]{3,2,0,1:T(8,128)}, u32[]{:S(2)}, u32[]{:S(2)}) collective-permute-start(f32[2,2,8,128]{3,2,0,1:T(8,128)} %bitcast.262), channel_id=1, source_target_pairs={{0,1},{2,3},{4,5},{6,7},{8,9},{10,11},{12,13},{14,15},{16,17},{18,... | collective-permute-start | bytes 49160 | tf_op jit(solution)/shard_map/ppermute | solution.py:23
  10.0 4.2 %copy-start.23 = (s32[8,32,128]{2,1,0:T(8,128)S(1)}, s32[8,32,128]{2,1,0:T(8,128)}, u32[]{:S(2)}) copy-start(s32[8,32,128]{2,1,0:T(8,128)} %param.8) | copy-start | bytes 393220
  19.7 1.4 %copy-start.20 = (f32[2,3,8,32,128]{4,3,2,1,0:T(8,128)S(1)}, f32[2,3,8,32,128]{4,3,2,1,0:T(8,128)}, u32[]{:S(2)}) copy-start(f32[2,3,8,32,128]{4,3,2,1,0:T(8,128)} %param.5) | copy-start | bytes 2359300
  24.8 5.1 %copy-start.21 = (f32[8,32,128]{2,1,0:T(8,128)S(1)}, f32[8,32,128]{2,1,0:T(8,128)}, u32[]{:S(2)}) copy-start(f32[8,32,128]{2,1,0:T(8,128)} %get-tuple-element.59) | copy-start | bytes 393220
  24.8 6.1 %collective-permute-start.5 = (f32[2,2,8,32]{3,2,0,1:T(8,128)S(1)}, f32[2,2,8,32]{3,2,0,1:T(8,128)S(1)}, u32[]{:S(2)}, u32[]{:S(2)}) collective-permute-start(f32[2,2,8,32]{3,2,0,1:T(8,128)S(1)} %bitcast.269), channel_id=1, source_target_pairs={{0,24},{8,0},{16,8},{24,16},{1,25},{9,1},{17,9},{25,17},{2,26},{10... | collective-permute-start | bytes 12296 | tf_op jit(solution)/shard_map/ppermute | solution.py:17
  27.1 5.6 %collective-permute-start.3 = (f32[2,2,32,128]{3,2,1,0:T(8,128)S(1)}, f32[2,2,32,128]{3,2,1,0:T(8,128)S(1)}, u32[]{:S(2)}, u32[]{:S(2)}) collective-permute-start(f32[2,2,32,128]{3,2,1,0:T(8,128)S(1)} %slice_bitcast_fusion.37), channel_id=1, source_target_pairs={{0,6},{2,0},{4,2},{6,4},{1,7},{3,1},{5,3},{7,5},{8,14},{10,8},{12,... | collective-permute-start | bytes 196616 | tf_op jit(solution)/shard_map/ppermute | solution.py:17
  28.6 4.1 %collective-permute-start.4 = (f32[2,2,8,128]{3,2,1,0:T(8,128)S(1)}, f32[2,2,8,128]{3,2,1,0:T(8,128)S(1)}, u32[]{:S(2)}, u32[]{:S(2)}) collective-permute-start(f32[2,2,8,128]{3,2,1,0:T(8,128)S(1)} %bitcast.271), channel_id=1, source_target_pairs={{1,0},{3,2},{5,4},{7,6},{9,8},{11,10},{13,12},{15,14},{17,16},{19,... | collective-permute-start | bytes 49160 | tf_op jit(solution)/shard_map/ppermute | solution.py:23
  42.6 5.6 %collective-permute-start.8 = (f32[2,2,8,32]{3,2,0,1:T(8,128)S(1)}, f32[2,2,8,32]{3,2,0,1:T(8,128)S(1)}, u32[]{:S(2)}, u32[]{:S(2)}) collective-permute-start(f32[2,2,8,32]{3,2,0,1:T(8,128)S(1)} %bitcast.270), channel_id=1, source_target_pairs={{0,8},{8,16},{16,24},{24,0},{1,9},{9,17},{17,25},{25,1},{2,10},{10... | collective-permute-start | bytes 12296 | tf_op jit(solution)/shard_map/ppermute | solution.py:17
  43.3 7.5 %collective-permute-start.6 = (f32[2,2,32,128]{3,2,0,1:T(8,128)}, f32[2,2,32,128]{3,2,0,1:T(8,128)}, u32[]{:S(2)}, u32[]{:S(2)}) collective-permute-start(f32[2,2,32,128]{3,2,0,1:T(8,128)} %copy_bitcast_fusion.2), channel_id=1, source_target_pairs={{0,2},{2,4},{4,6},{6,0},{1,3},{3,5},{5,7},{7,1},{8,10},{10,12},{12... | collective-permute-start | bytes 196616 | tf_op jit(solution)/shard_map/ppermute | solution.py:17
  44.7 5.3 %collective-permute-start.7 = (f32[2,2,8,128]{3,2,1,0:T(8,128)}, f32[2,2,8,128]{3,2,1,0:T(8,128)}, u32[]{:S(2)}, u32[]{:S(2)}) collective-permute-start(f32[2,2,8,128]{3,2,1,0:T(8,128)} %bitcast.264), channel_id=1, source_target_pairs={{0,1},{2,3},{4,5},{6,7},{8,9},{10,11},{12,13},{14,15},{16,17},{18,... | collective-permute-start | bytes 49160 | tf_op jit(solution)/shard_map/ppermute | solution.py:23
  50.0 1.7 %copy-start.12 = (f32[2,1,8,31,128]{4,3,0,2,1:T(8,128)S(1)}, f32[2,1,8,31,128]{4,3,0,2,1:T(8,128)}, u32[]{:S(2)}) copy-start(f32[2,1,8,31,128]{4,3,0,2,1:T(8,128)} %slice_bitcast_fusion.7) | copy-start | bytes 761860
  51.6 1.3 %copy-start.19 = (f32[2,1,7,32,128]{4,3,1,0,2:T(8,128)S(1)}, f32[2,1,7,32,128]{4,3,1,0,2:T(8,128)}, u32[]{:S(2)}) copy-start(f32[2,1,7,32,128]{4,3,1,0,2:T(8,128)} %slice_bitcast_fusion.30) | copy-start | bytes 688132
  51.7 1.2 %copy-start.13 = (f32[2,1,8,32,127]{4,3,0,2,1:T(8,128)S(1)}, f32[2,1,8,32,127]{4,3,0,2,1:T(8,128)}, u32[]{:S(2)}) copy-start(f32[2,1,8,32,127]{4,3,0,2,1:T(8,128)} %slice_bitcast_fusion.4) | copy-start | bytes 780292
  51.7 1.3 %copy-start.15 = (f32[2,1,8,31,128]{4,3,0,2,1:T(8,128)S(1)}, f32[2,1,8,31,128]{4,3,0,2,1:T(8,128)}, u32[]{:S(2)}) copy-start(f32[2,1,8,31,128]{4,3,0,2,1:T(8,128)} %slice_bitcast_fusion.6) | copy-start | bytes 761860
  51.7 1.3 %copy-start.16 = (f32[2,1,8,32,1]{4,3,1,0,2:T(8,128)S(1)}, f32[2,1,8,32,1]{4,3,1,0,2:T(8,128)}, u32[]{:S(2)}) copy-start(f32[2,1,8,32,1]{4,3,1,0,2:T(8,128)} %copy.1344) | copy-start | bytes 6148
  51.7 1.4 %copy-start.17 = (f32[2,1,8,32,1]{4,3,0,2,1:T(8,128)S(1)}, f32[2,1,8,32,1]{4,3,0,2,1:T(8,128)}, u32[]{:S(2)}) copy-start(f32[2,1,8,32,1]{4,3,0,2,1:T(8,128)} %copy.1347) | copy-start | bytes 6148
  60.7 5.6 %copy-start.3 = (f32[8,32,128]{1,0,2:T(8,128)S(1)}, f32[8,32,128]{1,0,2:T(8,128)}, u32[]{:S(2)}) copy-start(f32[8,32,128]{1,0,2:T(8,128)} %copy.1373) | copy-start | bytes 393220
  63.0 11.8 %collective-permute-start.11 = (f32[2,2,8,32]{3,2,0,1:T(8,128)S(1)}, f32[2,2,8,32]{3,2,0,1:T(8,128)S(1)}, u32[]{:S(2)}, u32[]{:S(2)}) collective-permute-start(f32[2,2,8,32]{3,2,0,1:T(8,128)S(1)} %bitcast.268), channel_id=1, source_target_pairs={{0,24},{8,0},{16,8},{24,16},{1,25},{9,1},{17,9},{25,17},{2,26},{10... | collective-permute-start | bytes 12296 | tf_op jit(solution)/shard_map/ppermute | solution.py:17
  70.4 6.3 %collective-permute-start.9 = (f32[2,2,32,128]{3,2,1,0:T(8,128)S(1)}, f32[2,2,32,128]{3,2,1,0:T(8,128)S(1)}, u32[]{:S(2)}, u32[]{:S(2)}) collective-permute-start(f32[2,2,32,128]{3,2,1,0:T(8,128)S(1)} %slice_bitcast_fusion.36), channel_id=1, source_target_pairs={{0,6},{2,0},{4,2},{6,4},{1,7},{3,1},{5,3},{7,5},{8,14},{10,8},{12,... | collective-permute-start | bytes 196616 | tf_op jit(solution)/shard_map/ppermute | solution.py:17
  73.5 3.1 %collective-permute-start.10 = (f32[2,2,8,128]{3,2,1,0:T(8,128)S(1)}, f32[2,2,8,128]{3,2,1,0:T(8,128)S(1)}, u32[]{:S(2)}, u32[]{:S(2)}) collective-permute-start(f32[2,2,8,128]{3,2,1,0:T(8,128)S(1)} %bitcast.272), channel_id=1, source_target_pairs={{1,0},{3,2},{5,4},{7,6},{9,8},{11,10},{13,12},{15,14},{17,16},{19,... | collective-permute-start | bytes 49160 | tf_op jit(solution)/shard_map/ppermute | solution.py:23
  77.7 1.7 %copy-start.2 = (f32[2,1,8,32,128]{4,3,1,0,2:T(8,128)S(1)}, f32[2,1,8,32,128]{4,3,1,0,2:T(8,128)}, u32[]{:S(2)}) copy-start(f32[2,1,8,32,128]{4,3,1,0,2:T(8,128)} %copy-done.1) | copy-start | bytes 786436
  (13 other events, 12.9 us)
where the time goes:
time: 82 us; the launch traced here: 80.6 us
  local copies, waits for them, and re-layouts  41.9 us (51%)
  starting transfers between devices  23.2 us (28%)
  other arithmetic  11.3 us (14%)
  between operations  3.89 us (5%)
    ppermute x8, starting transfers between devices, passed_along(): lax.ppermute(shard, axis, [(i, (i + by) % length) for i in range(length)])  15.6 us
    unnamed x58, local copies, waits for them, and re-layouts  11.3 us
    concatenate x26, local copies, waits for them, and re-layouts, neighbour_later(): return jnp.concatenate([inner, jnp.expand_dims(rim, axis)], axis=axis)  10.6 us
    concatenate x20, local copies, waits for them, and re-layouts, neighbour_prior(): return jnp.concatenate([jnp.expand_dims(rim, axis), inner], axis=axis)  8.97 us
    ppermute x4, starting transfers between devices, passed_along_2(): return lax.ppermute(block, axis, route)  7.64 us
    sub x2, other arithmetic, update_faces(): neighbour_later(e_zcomp, lead_y[:, 1], 1) - e_zcomp  3.18 us
    sub x2, other arithmetic, update_faces(): h_zcomp - neighbour_prior(h_zcomp, rim_y[:, 1], 1)  2.5 us
    slice x2, local copies, waits for them, and re-layouts, update_faces(): rim_x = passed_along(h_field[:, 1:3, :, :, -1], 'gx', 1)  2.32 us
  transfers between devices with their start and end apart: 12, of which 1 were waited for; matrix products, arithmetic and copies ran while one was open for 24% of the time, Pallas kernels for 0%

commit v1 on v0

v1 whole, which is shorter than its diff:
```python
import functools
import math

import jax
import jax.numpy as jnp
from jax import lax
from jax.experimental import pallas as pl
from jax.experimental.pallas import tpu as pltpu
from jax.sharding import PartitionSpec as P

time_step = 0.4
phase_x = 1.3
phase_y = 0.7
MESH = pl.DeviceIdType.MESH


def kernel(counts, eps, e_in, h_in, fwd_in, mat_in, e, h, g,
           fwd, mat, inv, xs, xr, yr, zs, zr, load_sem, send_sem, recv_sem):
    steps = fwd.shape[0]
    ny, nz, nx = mat.shape
    place = {a: lax.axis_index(a) for a in counts}
    after = {a: lax.rem(place[a] + 1, counts[a]) for a in counts}
    before = {a: lax.rem(place[a] + counts[a] - 1, counts[a]) for a in counts}

    loads = [
        pltpu.make_async_copy(h_in, h, load_sem.at[0]),
        pltpu.make_async_copy(e_in, e, load_sem.at[1]),
        pltpu.make_async_copy(mat_in, mat, load_sem.at[2]),
        pltpu.make_async_copy(fwd_in, fwd, load_sem.at[3]),
    ]
    for load in loads:
        load.start()

    barrier = pltpu.get_barrier_semaphore()
    greeted = 0
    for a in counts:
        pl.semaphore_signal(barrier, inc=1, device_id={a: after[a]}, device_id_type=MESH)
        greeted += 1
        if counts[a] > 2:
            pl.semaphore_signal(barrier, inc=1, device_id={a: before[a]}, device_id_type=MESH)
            greeted += 1
    pl.semaphore_wait(barrier, greeted)

    def remote(r, which, src, dst, axis):
        to = after[axis] if r % 2 == 0 else before[axis]
        return pltpu.make_async_remote_copy(
            src_ref=src, dst_ref=dst, send_sem=send_sem.at[r, which],
            recv_sem=recv_sem.at[r, which], device_id={axis: to}, device_id_type=MESH)

    def copies(r, field):
        edge = ny - 1 if r % 2 == 0 else 0
        return dict(
            x=remote(r, 0, xs.at[r], xr.at[r], "gx"),
            y0=remote(r, 1, field.at[:, 0, edge], yr.at[r, 0], "gy"),
            y1=remote(r, 2, field.at[:, 2, edge], yr.at[r, 1], "gy"),
            z=remote(r, 3, zs.at[r], zr.at[r], "gz"),
        )

    lane = lax.broadcasted_iota(jnp.int32, (nz, nx), 1)
    row = lax.broadcasted_iota(jnp.int32, (nz, nx), 0)
    half = 2 * ny

    def pack(packed, r, field, y):
        edge = nx - 1 if r % 2 == 0 else 0
        for s in range(2):
            for c in (1, 2):
                column = field[s, c, y][:, edge:edge + 1]
                packed = jnp.where(lane == (2 * s + c - 1) * ny + y, column, packed)
            last = nz - 1 if r % 2 == 0 else 0
            for c in (0, 1):
                zs[r, s, c, y:y + 1] = field[s, c, y, last:last + 1, :]
        return packed

    def rims(r):
        if r % 2 == 0:
            wx, wy, wz, sign = place["gx"] == 0, place["gy"] == 0, place["gz"] == 0, -1.0
        else:
            wx, wy, wz = (place[a] == counts[a] - 1 for a in ("gx", "gy", "gz"))
            sign = 1.0
        cx = jnp.where(wx, math.cos(phase_x), 1.0)
        sx = jnp.where(wx, sign * math.sin(phase_x), 0.0)
        cy = jnp.where(wy, math.cos(phase_y), 1.0)
        sy = jnp.where(wy, sign * math.sin(phase_y), 0.0)
        got = xr[r]
        other = jnp.where(lane < half, -pltpu.roll(got, nx - half, 1), pltpu.roll(got, half, 1))
        return got * cx + other * sx, cy, sy, wz

    def y_rim(r, i, cy, sy):
        a, b = yr[r, i, 0], yr[r, i, 1]
        return (a * cy - b * sy, a * sy + b * cy)

    def beside_x(v, r, packed, s, c, y):
        j = (2 * s + c - 1) * ny + y
        if r % 2 == 0:
            return jnp.where(lane == 0, packed[:, j:j + 1], pltpu.roll(v, 1, 1))
        return jnp.where(lane == nx - 1, packed[:, j:j + 1], pltpu.roll(v, nx - 1, 1))

    def beside_z(v, r, wz, s, c, y):
        rim = jnp.where(wz, 0.0, zr[r, s, c, y:y + 1, :])
        if r % 2 == 0:
            return jnp.where(row == 0, rim, pltpu.roll(v, 1, 0))
        return jnp.where(row == nz - 1, rim, pltpu.roll(v, nz - 1, 0))

    def curl(r, field, y, got, rim):
        packed, _, _, wz = got
        for s in range(2):
            fx, fy, fz = field[s, 0, y], field[s, 1, y], field[s, 2, y]
            if rim is None:
                near = y - 1 if r % 2 == 0 else y + 1
                fx_y, fz_y = field[s, 0, near], field[s, 2, near]
            else:
                fx_y, fz_y = rim[0][s], rim[1][s]
            fx_z = beside_z(fx, r, wz, s, 0, y)
            fy_z = beside_z(fy, r, wz, s, 1, y)
            fy_x = beside_x(fy, r, packed, s, 1, y)
            fz_x = beside_x(fz, r, packed, s, 2, y)
            yield s, 0, (fz - fz_y) - (fy - fy_z)
            yield s, 1, (fx - fx_z) - (fz - fz_x)
            yield s, 2, (fy - fy_x) - (fx - fx_y)

    def update(r, source, target, y, got, rim):
        scale = time_step * inv[y] if r % 2 == 0 else time_step
        for s, c, value in curl(r, source, y, got, rim):
            target[s, c, y] = target[s, c, y] - scale * value

    rounds = 2 * steps
    now = copies(0, h_in)
    now["y0"].start()
    now["y1"].start()
    loads[0].wait()
    packed = jnp.zeros((nz, nx), jnp.float32)
    for y in range(ny):
        packed = pack(packed, 0, h, y)
    xs[0] = packed
    now["x"].start()
    now["z"].start()
    loads[2].wait()
    inverse = [1.0 / jnp.full((nz, nx), eps[m], jnp.float32) for m in range(eps.shape[0])]
    for y in range(ny):
        kind = mat[y]
        value = inverse[0]
        for m in range(1, eps.shape[0]):
            value = jnp.where(kind == m, inverse[m], value)
        inv[y] = value
    loads[1].wait()

    for r in range(rounds):
        source, target = (h, e) if r % 2 == 0 else (e, h)
        inner = range(1, ny) if r % 2 == 0 else range(ny - 1)
        outer = 0 if r % 2 == 0 else ny - 1
        now["x"].wait_recv()
        now["z"].wait_recv()
        got = rims(r)
        packed = jnp.zeros((nz, nx), jnp.float32)
        more = r + 1 < rounds
        for y in inner:
            update(r, source, target, y, got, None)
            if more:
                packed = pack(packed, r + 1, target, y)
        now["y0"].wait_recv()
        now["y1"].wait_recv()
        rim = [y_rim(r, i, got[1], got[2]) for i in range(2)]
        update(r, source, target, outer, got, rim)
        for name in now:
            now[name].wait_send()
        if more:
            now = copies(r + 1, target)
            now["y0"].start()
            now["y1"].start()
            xs[r + 1] = pack(packed, r + 1, target, outer)
            now["x"].start()
            now["z"].start()
        if r % 2 == 0:
            n = r // 2
            if n == 0:
                loads[3].wait()
            for y in range(ny):
                total = None
                for s in range(2):
                    for c in range(3):
                        term = e[s, c, y] * fwd[n, s, c, y].astype(jnp.float32)
                        total = term if total is None else total + term
                total = inv[y] * total
                g[y] = total if n == 0 else g[y] + total


def shards(counts, adj_e, adj_h, fwd_e, material, eps_table):
    ny, nz, nx = material.shape
    rounds = 2 * fwd_e.shape[0]
    hbm = pl.BlockSpec(memory_space=pltpu.HBM)
    vmem = pl.BlockSpec(memory_space=pltpu.VMEM)
    f32 = jnp.float32
    return pl.pallas_call(
        functools.partial(kernel, counts),
        out_shape=(
            pltpu.VMEM(adj_e.shape, f32),
            pltpu.VMEM(adj_h.shape, f32),
            pltpu.VMEM(material.shape, f32),
        ),
        in_specs=[pl.BlockSpec(memory_space=pltpu.SMEM), hbm, hbm, hbm, hbm],
        out_specs=(vmem, vmem, vmem),
        scratch_shapes=[
            pltpu.VMEM(fwd_e.shape, fwd_e.dtype),
            pltpu.VMEM(material.shape, material.dtype),
            pltpu.VMEM(material.shape, f32),
            pltpu.VMEM((rounds, nz, nx), f32),
            pltpu.VMEM((rounds, nz, nx), f32),
            pltpu.VMEM((rounds, 2, 2, nz, nx), f32),
            pltpu.VMEM((rounds, 2, 2, ny, nx), f32),
            pltpu.VMEM((rounds, 2, 2, ny, nx), f32),
            pltpu.SemaphoreType.DMA((4,)),
            pltpu.SemaphoreType.DMA((rounds, 4)),
            pltpu.SemaphoreType.DMA((rounds, 4)),
        ],
        compiler_params=pltpu.CompilerParams(
            collective_id=0, has_side_effects=True, vmem_limit_bytes=24 * 1024 * 1024
        ),
    )(eps_table, adj_e, adj_h, fwd_e, material)


def solution(mesh):
    counts = {a: mesh.shape[a] for a in ("gx", "gy", "gz")}
    return jax.shard_map(
        functools.partial(shards, counts),
        mesh=mesh,
        in_specs=(
            P(None, None, "gy", "gz", "gx"),
            P(None, None, "gy", "gz", "gx"),
            P(None, None, None, "gy", "gz", "gx"),
            P("gy", "gz", "gx"),
            P(),
        ),
        out_specs=(
            P(None, None, "gy", "gz", "gx"),
            P(None, None, "gy", "gz", "gx"),
            P("gy", "gz", "gx"),
        ),
        check_vma=False,
    )
```

time: 82 us -> 32.3 us (0.39); the launches traced: 80.6 us -> 32 us
  local copies, waits for them, and re-layouts: 41.9 us -> 7.37 us
  Pallas kernels: 0 us -> 24 us
  starting transfers between devices: 23.2 us -> 0 us
  other arithmetic: 11.3 us -> 0 us
  between operations: 3.89 us -> 0.65 us
    pallas_call x0 -> x1, Pallas kernels: none -> 24 us  [shards(): pl.pallas_call(functools.partial(kernel, counts), out_shape=(pltpu.VMEM(a...]
    ppermute x12 -> x0, starting transfers between devices: 23.2 us -> none  [the longest x8 15.6 us: passed_along(): lax.ppermute(shard, axis, [(i, (i + by) % length) for i in range(length)])]
    concatenate x46 -> x0, local copies, waits for them, and re-layouts: 19.6 us -> none  [the longest x26 10.6 us: neighbour_later(): return jnp.concatenate([inner, jnp.expand_dims(rim, axis)], axis=axis)]
    slice x14 -> x0, local copies, waits for them, and re-layouts: 7.23 us -> none  [the longest x2 2.32 us: update_faces(): rim_x = passed_along(h_field[:, 1:3, :, :, -1], 'gx', 1)]
    sub x13 -> x0, other arithmetic: 6.79 us -> none  [the longest x2 3.18 us: update_faces(): neighbour_later(e_zcomp, lead_y[:, 1], 1) - e_zcomp]
    unnamed x58 -> x13, local copies, waits for them, and re-layouts: 11.3 us -> 7.37 us
    squeeze x11 -> x0, local copies, waits for them, and re-layouts: 3.72 us -> none  [the longest x2 1.53 us: update_faces(): lead_x = passed_along(e_field[:, 1:3, :, :, 0], 'gx', -1)]
    add x3 -> x0, other arithmetic: 2.45 us -> none  [the longest x1 2.01 us: shards(): grad_eps + inverse_eps * jnp.sum(e_field * fwd_e[section].astype(jnp.floa...]
  transfers between devices with their start and end apart: 12 -> 0, of which waited for: 1 -> 0; matrix products, arithmetic and copies ran while one was open for 24% -> 0% of each run, Pallas kernels for 0% -> 0%
where the time goes in v1:
time: 32.3 us; the launch traced here: 32 us
  Pallas kernels  24 us (74%)
  local copies, waits for them, and re-layouts  7.37 us (23%)
  between operations  0.65 us (2%)
    pallas_call x1, Pallas kernels, shards(): pl.pallas_call(functools.partial(kernel, counts), out_shape=(pltpu.VMEM(a...  24 us
    unnamed x13, local copies, waits for them, and re-layouts  7.37 us

profile of v1, /device:TPU:0, one launch (start us, length us, event | category | flops | bytes accessed | tf_op | source)
XLA Modules:
  0.0 32.0 jit_solution(6668607527662451937)
XLA Ops:
  0.6 0.0 copy-start
  0.6 1.1 %copy-done = f32[2,3,8,32,128]{4,3,2,1,0:T(8,128)S(1)} copy-done((f32[2,3,8,32,128]{4,3,2,1,0:T(8,128)S(1)}, f32[2,3,8,32,128]{4,3,2,1,0:T(8,128)}, u32[]{:S(2)}) %copy-start) | copy-done | bytes 786456
  1.8 0.0 copy-start.1
  1.8 1.1 %copy-done.1 = f32[2,3,8,32,128]{4,3,2,1,0:T(8,128)S(1)} copy-done((f32[2,3,8,32,128]{4,3,2,1,0:T(8,128)S(1)}, f32[2,3,8,32,128]{4,3,2,1,0:T(8,128)}, u32[]{:S(2)}) %copy-start.1) | copy-done | bytes 786456
  2.9 0.0 copy-start.2
  2.9 1.1 %copy-done.2 = bf16[2,2,3,8,32,128]{5,4,3,2,1,0:T(8,128)(2,1)S(1)} copy-done((bf16[2,2,3,8,32,128]{5,4,3,2,1,0:T(8,128)(2,1)S(1)}, bf16[2,2,3,8,32,128]{5,4,3,2,1,0:T(8,128)(2,1)}, u32[]{:S(2)}) %copy-start.2) | copy-done | bytes 786456
  4.0 0.0 copy-start.3
  4.0 0.9 %copy-done.3 = s32[8,32,128]{2,1,0:T(8,128)S(1)} copy-done((s32[8,32,128]{2,1,0:T(8,128)S(1)}, s32[8,32,128]{2,1,0:T(8,128)}, u32[]{:S(2)}) %copy-start.3) | copy-done | bytes 131096
  4.9 0.0 copy-start.4
  4.9 0.7 %copy-done.4 = f32[4]{0:T(128)S(1)} copy-done((f32[4]{0:T(128)S(1)}, f32[4]{0:T(128)}, u32[]{:S(2)}) %copy-start.4) | copy-done | bytes 40
  5.6 24.0 %shard_map.76 = (f32[2,3,8,32,128]{4,3,2,1,0:T(8,128)S(1)}, f32[2,3,8,32,128]{4,3,2,1,0:T(8,128)S(1)}, f32[8,32,128]{2,1,0:T(8,128)S(1)}) custom-call(f32[4]{0:T(128)S(1)} %copy-done.4, f32[2,3,8,32,128]{4,3,2,1,0:T(8,128)S(1)} %copy-done, f32[2,3,8,32,128]{4,3,2,1,0:T(8,128)S(1)} %copy-done.1, bf16[2,2,3,8,32,128]{5,4,3,2,1,0:T(8,128)(2,1)S(1)} %copy-done.2, ...), custom_call_target="tpu_custom_call" | custom-call | tf_op jit(solution)/shard_map/pallas_call | solution.py:193
  29.6 0.9 %copy.11 = f32[2,3,8,32,128]{4,3,2,1,0:T(8,128)} copy(f32[2,3,8,32,128]{4,3,2,1,0:T(8,128)S(1)} %get-tuple-element.3) | data formatting | bytes 1572864
  30.5 0.7 %copy.13 = f32[8,32,128]{2,1,0:T(8,128)} copy(f32[8,32,128]{2,1,0:T(8,128)S(1)} %get-tuple-element.5) | data formatting | bytes 262144
  31.1 0.9 %copy.12 = f32[2,3,8,32,128]{4,3,2,1,0:T(8,128)} copy(f32[2,3,8,32,128]{4,3,2,1,0:T(8,128)S(1)} %get-tuple-element.4) | data formatting | bytes 1572864
Async XLA Ops:
  0.6 1.1 %copy-start = (f32[2,3,8,32,128]{4,3,2,1,0:T(8,128)S(1)}, f32[2,3,8,32,128]{4,3,2,1,0:T(8,128)}, u32[]{:S(2)}) copy-start(f32[2,3,8,32,128]{4,3,2,1,0:T(8,128)} %e_in.1) | copy-start | bytes 2359300
  1.8 1.1 %copy-start.1 = (f32[2,3,8,32,128]{4,3,2,1,0:T(8,128)S(1)}, f32[2,3,8,32,128]{4,3,2,1,0:T(8,128)}, u32[]{:S(2)}) copy-start(f32[2,3,8,32,128]{4,3,2,1,0:T(8,128)} %h_in.1) | copy-start | bytes 2359300
  2.9 1.1 %copy-start.2 = (bf16[2,2,3,8,32,128]{5,4,3,2,1,0:T(8,128)(2,1)S(1)}, bf16[2,2,3,8,32,128]{5,4,3,2,1,0:T(8,128)(2,1)}, u32[]{:S(2)}) copy-start(bf16[2,2,3,8,32,128]{5,4,3,2,1,0:T(8,128)(2,1)} %fwd_in.1) | copy-start | bytes 2359300
  4.0 0.9 %copy-start.3 = (s32[8,32,128]{2,1,0:T(8,128)S(1)}, s32[8,32,128]{2,1,0:T(8,128)}, u32[]{:S(2)}) copy-start(s32[8,32,128]{2,1,0:T(8,128)} %mat_in.1) | copy-start | bytes 393220
  4.9 0.7 %copy-start.4 = (f32[4]{0:T(128)S(1)}, f32[4]{0:T(128)}, u32[]{:S(2)}) copy-start(f32[4]{0:T(128)} %eps.1) | copy-start | bytes 52

commit v2 on v1

--- a/solution.py
+++ b/solution.py
@@ -14,8 +14,55 @@
 MESH = pl.DeviceIdType.MESH
 
 
-def kernel(counts, eps, e_in, h_in, fwd_in, mat_in, e, h, g,
-           fwd, mat, inv, xs, xr, yr, zs, zr, load_sem, send_sem, recv_sem):
+def difference(field, s, y, lift, ahead_x, ahead_z):
+    fx, fy, fz = field[s, 0, y], field[s, 1, y], field[s, 2, y]
+    fx_y, fz_y = lift(s, y)
+    return (
+        (fz - fz_y) - (fy - ahead_z(fy, s, 1, y)),
+        (fx - ahead_z(fx, s, 0, y)) - (fz - ahead_x(fz, s, 2, y)),
+        (fy - ahead_x(fy, s, 1, y)) - (fx - fx_y),
+    )
+
+
+def finish(e_in, g_in, h_in, px, ry, rz, e_out, h_out, g_out, h, sem):
+    ny, nz, nx = g_in.shape
+    out = [pltpu.make_async_copy(e_in, e_out, sem.at[0]), pltpu.make_async_copy(g_in, g_out, sem.at[1])]
+    for copy in out:
+        copy.start()
+    lane = lax.broadcasted_iota(jnp.int32, (nz, nx), 1)
+    row = lax.broadcasted_iota(jnp.int32, (nz, nx), 0)
+    packed = px[...]
+
+    def lift(s, y):
+        if y == ny - 1:
+            return ry[0, s], ry[1, s]
+        return e_in[s, 0, y + 1], e_in[s, 2, y + 1]
+
+    def ahead_x(v, s, c, y):
+        j = (2 * s + c - 1) * ny + y
+        return jnp.where(lane == nx - 1, packed[:, j:j + 1], pltpu.roll(v, nx - 1, 1))
+
+    def ahead_z(v, s, c, y):
+        return jnp.where(row == nz - 1, rz[s, c, y:y + 1, :], pltpu.roll(v, nz - 1, 0))
+
+    block = ny // 2
+    for y in range(ny):
+        for s in range(2):
+            value = difference(e_in, s, y, lift, ahead_x, ahead_z)
+            for c in range(3):
+                h[s, c, y] = h_in[s, c, y] - time_step * value[c]
+        if (y + 1) % block == 0:
+            k = y // block
+            layers = pl.ds(k * block, block)
+            copy = pltpu.make_async_copy(h.at[:, :, layers], h_out.at[:, :, layers], sem.at[2 + k])
+            copy.start()
+            out.append(copy)
+    for copy in out:
+        copy.wait()
+
+
+def kernel(counts, eps_in, e_in, h_in, fwd_in, mat_in, e, h, g, px, ry, rz,
+           eps, fwd, mat, inv, xs, xr, yr, zs, zr, load_sem, send_sem, recv_sem):
     steps = fwd.shape[0]
     ny, nz, nx = mat.shape
     place = {a: lax.axis_index(a) for a in counts}
@@ -27,6 +74,7 @@
         pltpu.make_async_copy(e_in, e, load_sem.at[1]),
         pltpu.make_async_copy(mat_in, mat, load_sem.at[2]),
         pltpu.make_async_copy(fwd_in, fwd, load_sem.at[3]),
+        pltpu.make_async_copy(eps_in, eps, load_sem.at[4]),
     ]
     for load in loads:
         load.start()
@@ -101,27 +149,26 @@
             return jnp.where(row == 0, rim, pltpu.roll(v, 1, 0))
         return jnp.where(row == nz - 1, rim, pltpu.roll(v, nz - 1, 0))
 
-    def curl(r, field, y, got, rim):
+    def update(r, source, target, y, got, rim):
         packed, _, _, wz = got
+        scale = time_step * inv[y] if r % 2 == 0 else time_step
+
+        def lift(s, y):
+            if rim is not None:
+                return rim[0][s], rim[1][s]
+            near = y - 1 if r % 2 == 0 else y + 1
+            return source[s, 0, near], source[s, 2, near]
+
+        def side_x(v, s, c, y):
+            return beside_x(v, r, packed, s, c, y)
+
+        def side_z(v, s, c, y):
+            return beside_z(v, r, wz, s, c, y)
+
         for s in range(2):
-            fx, fy, fz = field[s, 0, y], field[s, 1, y], field[s, 2, y]
-            if rim is None:
-                near = y - 1 if r % 2 == 0 else y + 1
-                fx_y, fz_y = field[s, 0, near], field[s, 2, near]
-            else:
-                fx_y, fz_y = rim[0][s], rim[1][s]
-            fx_z = beside_z(fx, r, wz, s, 0, y)
-            fy_z = beside_z(fy, r, wz, s, 1, y)
-            fy_x = beside_x(fy, r, packed, s, 1, y)
-            fz_x = beside_x(fz, r, packed, s, 2, y)
-            yield s, 0, (fz - fz_y) - (fy - fy_z)
-            yield s, 1, (fx - fx_z) - (fz - fz_x)
-            yield s, 2, (fy - fy_x) - (fx - fx_y)
-
-    def update(r, source, target, y, got, rim):
-        scale = time_step * inv[y] if r % 2 == 0 else time_step
-        for s, c, value in curl(r, source, y, got, rim):
-            target[s, c, y] = target[s, c, y] - scale * value
+            value = difference(source, s, y, lift, side_x, side_z)
+            for c in range(3):
+                target[s, c, y] = target[s, c, y] - scale * value[c]
 
     rounds = 2 * steps
     now = copies(0, h_in)
@@ -135,6 +182,7 @@
     now["x"].start()
     now["z"].start()
     loads[2].wait()
+    loads[4].wait()
     inverse = [1.0 / jnp.full((nz, nx), eps[m], jnp.float32) for m in range(eps.shape[0])]
     for y in range(ny):
         kind = mat[y]
@@ -151,25 +199,34 @@
         now["x"].wait_recv()
         now["z"].wait_recv()
         got = rims(r)
+        if r == rounds - 1:
+            px[...] = got[0]
+            for s in range(2):
+                for c in range(2):
+                    rz[s, c] = jnp.where(got[3], 0.0, zr[r, s, c])
+            now["y0"].wait_recv()
+            now["y1"].wait_recv()
+            for i in range(2):
+                ry[i, 0], ry[i, 1] = y_rim(r, i, got[1], got[2])
+            for name in now:
+                now[name].wait_send()
+            break
         packed = jnp.zeros((nz, nx), jnp.float32)
-        more = r + 1 < rounds
         for y in inner:
             update(r, source, target, y, got, None)
-            if more:
-                packed = pack(packed, r + 1, target, y)
+            packed = pack(packed, r + 1, target, y)
         now["y0"].wait_recv()
         now["y1"].wait_recv()
         rim = [y_rim(r, i, got[1], got[2]) for i in range(2)]
         update(r, source, target, outer, got, rim)
         for name in now:
             now[name].wait_send()
-        if more:
-            now = copies(r + 1, target)
-            now["y0"].start()
-            now["y1"].start()
-            xs[r + 1] = pack(packed, r + 1, target, outer)
-            now["x"].start()
-            now["z"].start()
+        now = copies(r + 1, target)
+        now["y0"].start()
+        now["y1"].start()
+        xs[r + 1] = pack(packed, r + 1, target, outer)
+        now["x"].start()
+        now["z"].start()
         if r % 2 == 0:
             n = r // 2
             if n == 0:
@@ -190,16 +247,20 @@
     hbm = pl.BlockSpec(memory_space=pltpu.HBM)
     vmem = pl.BlockSpec(memory_space=pltpu.VMEM)
     f32 = jnp.float32
-    return pl.pallas_call(
+    e, h, g, px, ry, rz = pl.pallas_call(
         functools.partial(kernel, counts),
         out_shape=(
             pltpu.VMEM(adj_e.shape, f32),
             pltpu.VMEM(adj_h.shape, f32),
             pltpu.VMEM(material.shape, f32),
-        ),
-        in_specs=[pl.BlockSpec(memory_space=pltpu.SMEM), hbm, hbm, hbm, hbm],
-        out_specs=(vmem, vmem, vmem),
+            pltpu.VMEM((nz, nx), f32),
+            pltpu.VMEM((2, 2, nz, nx), f32),
+            pltpu.VMEM((2, 2, ny, nx), f32),
+        ),
+        in_specs=[hbm] * 5,
+        out_specs=[vmem] * 6,
         scratch_shapes=[
+            pltpu.SMEM(eps_table.shape, f32),
             pltpu.VMEM(fwd_e.shape, fwd_e.dtype),
             pltpu.VMEM(material.shape, material.dtype),
             pltpu.VMEM(material.shape, f32),
@@ -208,14 +269,26 @@
             pltpu.VMEM((rounds, 2, 2, nz, nx), f32),
             pltpu.VMEM((rounds, 2, 2, ny, nx), f32),
             pltpu.VMEM((rounds, 2, 2, ny, nx), f32),
-            pltpu.SemaphoreType.DMA((4,)),
+            pltpu.SemaphoreType.DMA((5,)),
             pltpu.SemaphoreType.DMA((rounds, 4)),
             pltpu.SemaphoreType.DMA((rounds, 4)),
         ],
         compiler_params=pltpu.CompilerParams(
             collective_id=0, has_side_effects=True, vmem_limit_bytes=24 * 1024 * 1024
         ),
-    )(eps_table, adj_e, adj_h, fwd_e, material)
+    )(*(pltpu.with_memory_space_constraint(a, pltpu.HBM) for a in (eps_table, adj_e, adj_h, fwd_e, material)))
+    return pl.pallas_call(
+        finish,
+        out_shape=(
+            jax.ShapeDtypeStruct(adj_e.shape, f32),
+            jax.ShapeDtypeStruct(adj_h.shape, f32),
+            jax.ShapeDtypeStruct(material.shape, f32),
+        ),
+        in_specs=[vmem] * 6,
+        out_specs=[hbm] * 3,
+        scratch_shapes=[pltpu.VMEM(adj_h.shape, f32), pltpu.SemaphoreType.DMA((4,))],
+        compiler_params=pltpu.CompilerParams(vmem_limit_bytes=8 * 1024 * 1024),
+    )(e, g, h, px, ry, rz)
 
 
 def solution(mesh):

time: 32.3 us -> 25 us (0.77)
  local copies, waits for them, and re-layouts: 7.37 us -> 0 us
    unnamed x13 -> x0, local copies, waits for them, and re-layouts: 7.37 us -> none
    pallas_call x0 -> x1, Pallas kernels: none -> 1.25 us  [shards(): pl.pallas_call(finish, out_shape=(jax.ShapeDtypeStruct(adj_e.shape, f32),...]
    pallas_call x1, Pallas kernels: 24 us -> 22.9 us  [shards(): pl.pallas_call(functools.partial(kernel, counts), out_shape=(pltpu.VMEM(a...]
where the time goes in v2:
time: 25 us; the launch traced here: 24.8 us
  Pallas kernels  24.2 us (97%)
  between operations  0.64 us (3%)
    pallas_call x1, Pallas kernels, shards(): pl.pallas_call(functools.partial(kernel, counts), out_shape=(pltpu.VMEM(a...  22.9 us
    pallas_call x1, Pallas kernels, shards(): pl.pallas_call(finish, out_shape=(jax.ShapeDtypeStruct(adj_e.shape, f32),...  1.25 us

profile of v2, /device:TPU:0, one launch (start us, length us, event | category | flops | bytes accessed | tf_op | source)
XLA Modules:
  0.0 24.8 jit_solution(14837789099351610613)
XLA Ops:
  0.6 22.9 %shard_map.76 = (f32[2,3,8,32,128]{4,3,2,1,0:T(8,128)S(1)}, f32[2,3,8,32,128]{4,3,2,1,0:T(8,128)S(1)}, f32[8,32,128]{2,1,0:T(8,128)S(1)}, f32[32,128]{1,0:T(8,12...) custom-call(f32[4]{0:T(128)} %eps_in.1, f32[2,3,8,32,128]{4,3,2,1,0:T(8,128)} %e_in.1, ...), custom_call_target="tpu_custom_call" | custom-call | tf_op jit(solution)/shard_map/pallas_call | solution.py:250
  23.6 1.2 %shard_map.77 = (f32[2,3,8,32,128]{4,3,2,1,0:T(8,128)}, f32[2,3,8,32,128]{4,3,2,1,0:T(8,128)}, f32[8,32,128]{2,1,0:T(8,128)}) custom-call(f32[2,3,8,32,128]{4,3,2,1,0:T(8,128)S(1)} %get-tuple-element.9.e_in, f32[8,32,128]{2,1,0:T(8,128)S(1)} %get-tuple-element.10.g_in, f32[2,3,8,32,128]{4,3,2,1,0:T(8,128)S(1)} %get-tuple-element.11.h_in, ...), custom_call_target="tpu_custom_call" | custom-call | tf_op jit(solution)/shard_map/pallas_call | solution.py:280

commit v3 on v2

v3 whole, which is shorter than its diff:
```python
import functools
import math

import jax
import jax.numpy as jnp
from jax import lax
from jax.experimental import pallas as pl
from jax.experimental.pallas import tpu as pltpu
from jax.sharding import PartitionSpec as P

time_step = 0.4
phase_x = 1.3
phase_y = 0.7
MESH = pl.DeviceIdType.MESH


def difference(field, s, y, lift, ahead_x, ahead_z):
    fx, fy, fz = field[s, 0, y], field[s, 1, y], field[s, 2, y]
    fx_y, fz_y = lift(s, y)
    return (
        (fz - fz_y) - (fy - ahead_z(fy, s, 1, y)),
        (fx - ahead_z(fx, s, 0, y)) - (fz - ahead_x(fz, s, 2, y)),
        (fy - ahead_x(fy, s, 1, y)) - (fx - fx_y),
    )


def finish(e_in, g_in, h_in, px, ry, rz, e_out, h_out, g_out, h, sem):
    ny, nz, nx = g_in.shape
    out = [pltpu.make_async_copy(e_in, e_out, sem.at[0]), pltpu.make_async_copy(g_in, g_out, sem.at[1])]
    for copy in out:
        copy.start()
    lane = lax.broadcasted_iota(jnp.int32, (nz, nx), 1)
    row = lax.broadcasted_iota(jnp.int32, (nz, nx), 0)

    def lift(s, y):
        if y == ny - 1:
            return ry[0, s], ry[1, s]
        return e_in[s, 0, y + 1], e_in[s, 2, y + 1]

    def ahead_x(v, s, c, y):
        j = s * ny + y
        return jnp.where(lane == nx - 1, px[c - 1][:, j:j + 1], pltpu.roll(v, nx - 1, 1))

    def ahead_z(v, s, c, y):
        return jnp.where(row == nz - 1, rz[s, c, y:y + 1, :], pltpu.roll(v, nz - 1, 0))

    block = ny // 2
    for y in range(ny):
        for s in range(2):
            value = difference(e_in, s, y, lift, ahead_x, ahead_z)
            for c in range(3):
                h[s, c, y] = h_in[s, c, y] - time_step * value[c]
        if (y + 1) % block == 0:
            k = y // block
            layers = pl.ds(k * block, block)
            copy = pltpu.make_async_copy(h.at[:, :, layers], h_out.at[:, :, layers], sem.at[2 + k])
            copy.start()
            out.append(copy)
    for copy in out:
        copy.wait()


FACES = (
    ("xp", (1, 0, 0)), ("xm", (-1, 0, 0)), ("yp0", (0, 1, 0)), ("yp2", (0, 1, 0)),
    ("ym", (0, -1, 0)), ("zp", (0, 0, 1)), ("zm", (0, 0, -1)),
)
EDGES = (
    ("ymzp", (0, -1, 1)), ("ymxp", (1, -1, 0)), ("xmzp", (-1, 0, 1)),
    ("xmyp", (-1, 1, 0)), ("zmyp", (0, 1, -1)), ("zmxp", (1, 0, -1)),
)
FIRST = (
    ("ey0", (0, -1, 0)), ("ey2", (0, -1, 0)), ("em", (0, -1, 0)), ("ex", (-1, 0, 0)), ("ez", (0, 0, -1)),
)
SENDS = FACES + EDGES + FIRST


def kernel(counts, eps_in, e_in, h_in, fwd_in, mat_in, e, h, g, px, ry, rz,
           eps, fwd, mat, inv, kx, ky, kz,
           xp, xp_s, xm_s, ed, zp, zm, xp_r, xm_r, yp_r, ym_r, zp_r, zm_r,
           ymzp_r, ymxp_r, xmzp_r, xmyp_r, zmyp_r, zmxp_r,
           ex, ez, ex_r, ey_r, em_r, ez_r, load_sem, send_sem, recv_sem):
    steps = fwd.shape[0]
    ny, nz, nx = mat.shape
    axes = ("gx", "gy", "gz")
    place = {a: lax.axis_index(a) for a in axes}

    def at(offset):
        return {a: lax.rem(place[a] + (o % counts[a]), counts[a]) for a, o in zip(axes, offset)}

    near = []
    for _, offset in FACES + EDGES:
        for sign in (1, -1):
            o = tuple(sign * v % counts[a] for a, v in zip(axes, offset))
            if o not in near and any(o):
                near.append(o)
    barrier = pltpu.get_barrier_semaphore()
    for o in near:
        pl.semaphore_signal(barrier, inc=1, device_id=at(o), device_id_type=MESH)
    loads = [
        pltpu.make_async_copy(h_in, h, load_sem.at[0]),
        pltpu.make_async_copy(e_in, e, load_sem.at[1]),
        pltpu.make_async_copy(mat_in, mat, load_sem.at[2]),
        pltpu.make_async_copy(eps_in, eps, load_sem.at[4]),
        pltpu.make_async_copy(fwd_in, fwd, load_sem.at[3]),
    ]
    for load in loads:
        load.start()
    load_h, load_e, load_mat, load_eps, load_fwd = loads

    pl.semaphore_wait(barrier, len(near))

    def copies(n):
        field = h_in if n == 0 else h
        ends = dict(
            xp=(xp_s.at[n], xp_r.at[n]),
            xm=(xm_s.at[n], xm_r.at[n]),
            yp0=(field.at[:, 0, ny - 1], yp_r.at[n, 0]),
            yp2=(field.at[:, 2, ny - 1], yp_r.at[n, 1]),
            ym=(field.at[:, :, 0], ym_r.at[n]),
            zp=(zp.at[n], zp_r.at[n]),
            zm=(zm.at[n], zm_r.at[n]),
            ymzp=(ed.at[n], ymzp_r.at[n]),
            ymxp=(xp_s.at[n], ymxp_r.at[n]),
            xmzp=(xm_s.at[n, 1], xmzp_r.at[n]),
            xmyp=(xm_s.at[n, 1], xmyp_r.at[n]),
            zmyp=(ed.at[n], zmyp_r.at[n]),
            zmxp=(xp_s.at[n], zmxp_r.at[n]),
        )
        if n == 0:
            ends.update(
                ey0=(e_in.at[:, 0, 0], ey_r.at[0]),
                ey2=(e_in.at[:, 2, 0], ey_r.at[1]),
                em=(mat_in.at[0], em_r),
                ex=(ex, ex_r),
                ez=(ez, ez_r),
            )
        return {
            name: pltpu.make_async_remote_copy(
                src_ref=ends[name][0], dst_ref=ends[name][1], send_sem=send_sem.at[n, i],
                recv_sem=recv_sem.at[n, i], device_id=at(offset), device_id_type=MESH)
            for i, (name, offset) in enumerate(SENDS) if name in ends
        }

    lane = lax.broadcasted_iota(jnp.int32, (nz, nx), 1)
    row = lax.broadcasted_iota(jnp.int32, (nz, nx), 0)
    lane8, row8 = lane[:ny], row[:ny]
    blank = jnp.zeros((nz, nx), jnp.float32)

    def turn(axis, place_of_wrap, phase):
        wraps = place[axis] == place_of_wrap
        return jnp.where(wraps, math.cos(phase), 1.0), jnp.where(wraps, math.sin(phase), 0.0)

    x_behind, x_ahead = turn("gx", 0, -phase_x), turn("gx", counts["gx"] - 1, phase_x)
    y_behind, y_ahead = turn("gy", 0, -phase_y), turn("gy", counts["gy"] - 1, phase_y)
    z_first, z_last = place["gz"] == 0, place["gz"] == counts["gz"] - 1

    def rot(a, b, by):
        return a * by[0] - b * by[1], a * by[1] + b * by[0]

    def rot_packed(v, by):
        index = lax.broadcasted_iota(jnp.int32, v.shape, 1)
        other = jnp.where(index < ny, -pltpu.roll(v, nx - ny, 1), pltpu.roll(v, ny, 1))
        return v * by[0] + other * by[1]

    tiles = nz // 8
    width = nx // tiles

    def fold(a, b):
        v = a if b is None else a + pltpu.roll(b, 2 * ny, 1)
        total = v[0:8]
        for k in range(1, tiles):
            total = total + pltpu.roll(v[8 * k:8 * k + 8], k * width, 1)
        return total

    def unfold(v):
        a = jnp.concatenate([v] + [pltpu.roll(v, nx - k * width, 1) for k in range(1, tiles)], 0)
        return a, pltpu.roll(a, nx - 2 * ny, 1)

    def put(packed, column, y, s):
        return jnp.where(lane == s * ny + y, column, packed)

    def pack(packed, n, y):
        packed = list(packed)
        for s in range(2):
            for c in range(3):
                v = h[s, c, y]
                if c > 0:
                    packed[c - 1] = put(packed[c - 1], v[:, nx - 1:nx], y, s)
                packed[2 + c] = put(packed[2 + c], v[:, 0:1], y, s)
                if c < 2:
                    zp[n, s, c, y:y + 1] = h[s, c, y, nz - 1:nz, :]
                zm[n, s, c, y:y + 1] = h[s, c, y, 0:1, :]
        return packed

    def store_packed(packed, n):
        for i in range(2):
            xp[n, i] = packed[i]
        xp_s[n] = fold(packed[0], packed[1])
        xm_s[n, 0] = fold(packed[3], packed[4])
        xm_s[n, 1] = fold(packed[2], None)
        for s in range(2):
            ed[n, s:s + 1] = h[s, 1, 0, nz - 1:nz, :]
            ed[n, 2 + s:3 + s] = h[s, 2, ny - 1, 0:1, :]
        ed[n, 4:8] = jnp.zeros((4, nx), jnp.float32)

    def start(now, *names):
        for name in names:
            now[name].start()

    def landed(now, *names):
        for name in names:
            now[name].wait_recv()

    def shift(v, before, axis):
        index = lax.broadcasted_iota(jnp.int32, v.shape, axis)
        return jnp.where(index == 0, before, pltpu.roll(v, 1, axis))

    def update_e(n, y, xb, yb):
        scale = time_step * inv[y]

        def lift(s, y):
            if yb is not None:
                return yb[0][s], yb[1][s]
            return h[s, 0, y - 1], h[s, 2, y - 1]

        def side_x(v, s, c, y):
            j = s * ny + y
            return shift(v, xb[c - 1][:, j:j + 1], 1)

        def side_z(v, s, c, y):
            return shift(v, jnp.where(z_first, 0.0, zp_r[n, s, c, y:y + 1, :]), 0)

        for s in range(2):
            value = difference(h, s, y, lift, side_x, side_z)
            for c in range(3):
                e[s, c, y] = e[s, c, y] - scale * value[c]

    def update_h(y):
        def lift(s, y):
            if y == ny - 1:
                return ry[0, s], ry[1, s]
            return e[s, 0, y + 1], e[s, 2, y + 1]

        def side_x(v, s, c, y):
            j = s * ny + y
            return jnp.where(lane == nx - 1, px[c - 1][:, j:j + 1], pltpu.roll(v, nx - 1, 1))

        def side_z(v, s, c, y):
            return jnp.where(row == nz - 1, rz[s, c, y:y + 1, :], pltpu.roll(v, nz - 1, 0))

        for s in range(2):
            value = difference(e, s, y, lift, side_x, side_z)
            for c in range(3):
                h[s, c, y] = h[s, c, y] + -time_step * value[c]

    def front_x(n):
        hx, hy, hz = (rot_packed(v, x_ahead) for v in (unfold(xm_r[n, 1])[0], *unfold(xm_r[n, 0])))
        below = jnp.where(z_first, 0.0, rot_packed(unfold(xmzp_r[n])[0], x_ahead)[nz - 1:nz, :])
        hx_z = shift(hx, below, 0)
        side = rot_packed(rot_packed(unfold(xmyp_r[n])[0], x_ahead), y_behind)
        side = pltpu.roll(side, nx - (ny - 1), 1)
        first = jnp.logical_or(lane == 0, lane == ny)
        hx_y = jnp.where(first, side, pltpu.roll(hx, 1, 1))
        scale = time_step * kx[...]
        px[0] = px[0] - scale * ((hx - hx_z) - (hz - xp[n, 1]))
        px[1] = px[1] - scale * ((hy - xp[n, 0]) - (hx - hx_y))

    def front_z(n):
        scale = time_step * kz[...]
        side = rot(zmyp_r[n, 2:3, :], zmyp_r[n, 3:4, :], y_behind)
        corner = rot_packed(unfold(zmxp_r[n])[1], x_behind)[0:1, :]
        for s in range(2):
            hx, hy, hz = (zm_r[n, s, c] for c in range(3))
            hz_y = shift(hz, side[s], 0)
            column = jnp.sum(jnp.where(lane8 == s * ny + row8, corner, 0.0), axis=1, keepdims=True)
            hz_x = shift(hz, column, 1)
            e_x = rz[s, 0] - scale * ((hz - hz_y) - (hy - zp[n, s, 1]))
            e_y = rz[s, 1] - scale * ((hx - zp[n, s, 0]) - (hz - hz_x))
            rz[s, 0] = jnp.where(z_last, 0.0, e_x)
            rz[s, 1] = jnp.where(z_last, 0.0, e_y)

    def front_y(n):
        scale = time_step * ky[...]
        ahead = [rot(ym_r[n, 0, c], ym_r[n, 1, c], y_ahead) for c in range(3)]
        below = rot(ymzp_r[n, 0:1, :], ymzp_r[n, 1:2, :], y_ahead)
        corner = rot_packed(rot_packed(unfold(ymxp_r[n])[0], y_ahead), x_behind)
        for s in range(2):
            hx, hy, hz = (ahead[c][s] for c in range(3))
            hy_z = shift(hy, jnp.where(z_first, 0.0, below[s]), 0)
            hy_x = shift(hy, corner[:, s * ny:s * ny + 1], 1)
            ry[0, s] = ry[0, s] - scale * ((hz - h[s, 2, ny - 1]) - (hy - hy_z))
            ry[1, s] = ry[1, s] - scale * ((hy - hy_x) - (hx - h[s, 0, ny - 1]))

    def gradient(n):
        for y in range(ny):
            total = None
            for s in range(2):
                for c in range(3):
                    term = e[s, c, y] * fwd[n, s, c, y].astype(jnp.float32)
                    total = term if total is None else total + term
            total = inv[y] * total
            g[y] = total if n == 0 else g[y] + total

    now = copies(0)
    start(now, "yp0", "yp2", "ym", "em", "ey0", "ey2")
    load_h.wait()
    packed = [blank] * 5
    for y in range(ny):
        packed = pack(packed, 0, y)
    store_packed(packed, 0)
    start(now, "xp", "zp", "xm", "zm")
    start(now, *(name for name, _ in EDGES))
    load_mat.wait()
    load_eps.wait()
    table = [1.0 / jnp.full((nz, nx), eps[m], jnp.float32) for m in range(eps.shape[0])]

    def inverse(kind):
        value = table[0]
        for m in range(1, eps.shape[0]):
            value = jnp.where(kind == m, table[m], value)
        return value

    for y in range(ny):
        inv[y] = inverse(mat[y])
    load_e.wait()
    packed = [blank] * 3
    for y in range(ny):
        for s in range(2):
            for c in (1, 2):
                packed[c - 1] = put(packed[c - 1], e[s, c, y][:, 0:1], y, s)
            packed[2] = put(packed[2], inv[y][:, 0:1], y, s)
            for c in (0, 1):
                ez[2 * s + c, y:y + 1] = e[s, c, y, 0:1, :]
        ez[4, y:y + 1] = inv[y, 0:1, :]
    ex[0] = fold(packed[0], packed[1])
    ex[1] = fold(packed[2], None)
    start(now, "ex", "ez")

    for n in range(steps):
        landed(now, "xp", "zp")
        xb = [rot_packed(v, x_behind) for v in unfold(xp_r[n])]
        for y in range(1, ny):
            update_e(n, y, xb, None)
        landed(now, "yp0", "yp2")
        update_e(n, 0, xb, [rot(yp_r[n, i, 0], yp_r[n, i, 1], y_behind) for i in range(2)])
        if n == steps - 1:
            if n == 0:
                load_fwd.wait()
            gradient(n)
        if n == 0:
            landed(now, "ex", "ez", "em", "ey0", "ey2")
            ex_u = unfold(ex_r[0])
            for i in range(2):
                px[i] = rot_packed(ex_u[i], x_ahead)
                ry[i, 0], ry[i, 1] = rot(ey_r[i, 0], ey_r[i, 1], y_ahead)
                for c in range(2):
                    rz[i, c] = ez_r[2 * i + c]
            kx[...] = unfold(ex_r[1])[0]
            kz[...] = ez_r[4]
            ky[...] = inverse(em_r[...])
        landed(now, "xm", "zm", *(name for name, _ in EDGES))
        front_x(n)
        front_z(n)
        landed(now, "ym")
        front_y(n)
        for copy in now.values():
            copy.wait_send()
        if n == steps - 1:
            break
        packed = [blank] * 5
        later = copies(n + 1)
        for y in (0, ny - 1, *range(1, ny - 1)):
            update_h(y)
            packed = pack(packed, n + 1, y)
            if y == 0:
                later["ym"].start()
            if y == ny - 1:
                start(later, "yp0", "yp2")
        store_packed(packed, n + 1)
        start(later, "xp", "zp", "xm", "zm")
        start(later, *(name for name, _ in EDGES))
        now = later
        if n == 0:
            load_fwd.wait()
        gradient(n)


def shards(counts, adj_e, adj_h, fwd_e, material, eps_table):
    ny, nz, nx = material.shape
    steps = fwd_e.shape[0]
    hbm = pl.BlockSpec(memory_space=pltpu.HBM)
    vmem = pl.BlockSpec(memory_space=pltpu.VMEM)
    f32 = jnp.float32
    e, h, g, px, ry, rz = pl.pallas_call(
        functools.partial(kernel, counts),
        out_shape=(
            pltpu.VMEM(adj_e.shape, f32),
            pltpu.VMEM(adj_h.shape, f32),
            pltpu.VMEM(material.shape, f32),
            pltpu.VMEM((2, nz, nx), f32),
            pltpu.VMEM((2, 2, nz, nx), f32),
            pltpu.VMEM((2, 2, ny, nx), f32),
        ),
        in_specs=[hbm] * 5,
        out_specs=[vmem] * 6,
        scratch_shapes=[
            pltpu.SMEM(eps_table.shape, f32),
            pltpu.VMEM(fwd_e.shape, fwd_e.dtype),
            pltpu.VMEM(material.shape, material.dtype),
            pltpu.VMEM(material.shape, f32),
            pltpu.VMEM((nz, nx), f32),
            pltpu.VMEM((nz, nx), f32),
            pltpu.VMEM((ny, nx), f32),
            *(pltpu.VMEM((steps, *shape), f32) for shape in (
                (2, nz, nx), (8, nx), (2, 8, nx), (8, nx), (2, 2, ny, nx), (2, 3, ny, nx),
                (8, nx), (2, 8, nx), (2, 2, nz, nx), (2, 3, nz, nx),
                (2, 2, ny, nx), (2, 3, ny, nx), *[(8, nx)] * 6)),
            pltpu.VMEM((2, 8, nx), f32),
            pltpu.VMEM((5, ny, nx), f32),
            pltpu.VMEM((2, 8, nx), f32),
            pltpu.VMEM((2, 2, nz, nx), f32),
            pltpu.VMEM((nz, nx), material.dtype),
            pltpu.VMEM((5, ny, nx), f32),
            pltpu.SemaphoreType.DMA((5,)),
            pltpu.SemaphoreType.DMA((steps, len(SENDS))),
            pltpu.SemaphoreType.DMA((steps, len(SENDS))),
        ],
        compiler_params=pltpu.CompilerParams(
            collective_id=0, has_side_effects=True, vmem_limit_bytes=24 * 1024 * 1024
        ),
    )(*(pltpu.with_memory_space_constraint(a, pltpu.HBM) for a in (eps_table, adj_e, adj_h, fwd_e, material)))
    return pl.pallas_call(
        finish,
        out_shape=(
            jax.ShapeDtypeStruct(adj_e.shape, f32),
            jax.ShapeDtypeStruct(adj_h.shape, f32),
            jax.ShapeDtypeStruct(material.shape, f32),
        ),
        in_specs=[vmem] * 6,
        out_specs=[hbm] * 3,
        scratch_shapes=[pltpu.VMEM(adj_h.shape, f32), pltpu.SemaphoreType.DMA((4,))],
        compiler_params=pltpu.CompilerParams(vmem_limit_bytes=8 * 1024 * 1024),
    )(e, g, h, px, ry, rz)


def solution(mesh):
    counts = {a: mesh.shape[a] for a in ("gx", "gy", "gz")}
    return jax.shard_map(
        functools.partial(shards, counts),
        mesh=mesh,
        in_specs=(
            P(None, None, "gy", "gz", "gx"),
            P(None, None, "gy", "gz", "gx"),
            P(None, None, None, "gy", "gz", "gx"),
            P("gy", "gz", "gx"),
            P(),
        ),
        out_specs=(
            P(None, None, "gy", "gz", "gx"),
            P(None, None, "gy", "gz", "gx"),
            P("gy", "gz", "gx"),
        ),
        check_vma=False,
    )
```

time: 25 us -> 24.1 us (0.964)
  Pallas kernels: 24.2 us -> 23.3 us
    pallas_call x1, Pallas kernels: 22.9 us -> 22 us  [shards(): pl.pallas_call(functools.partial(kernel, counts), out_shape=(pltpu.VMEM(a...]
where the time goes in v3:
time: 24.1 us; the launch traced here: 23.9 us
  Pallas kernels  23.3 us (97%)
  between operations  0.64 us (3%)
    pallas_call x1, Pallas kernels, shards(): pl.pallas_call(functools.partial(kernel, counts), out_shape=(pltpu.VMEM(a...  22 us
    pallas_call x1, Pallas kernels, shards(): pl.pallas_call(finish, out_shape=(jax.ShapeDtypeStruct(adj_e.shape, f32),...  1.22 us

profile of v3, /device:TPU:0, one launch (start us, length us, event | category | flops | bytes accessed | tf_op | source)
XLA Modules:
  0.0 23.9 jit_solution(7438256910588267596)
XLA Ops:
  0.6 22.0 %shard_map.76 = (f32[2,3,8,32,128]{4,3,2,1,0:T(8,128)S(1)}, f32[2,3,8,32,128]{4,3,2,1,0:T(8,128)S(1)}, f32[8,32,128]{2,1,0:T(8,128)S(1)}, f32[2,32,128]{2,1,0:T(...) custom-call(f32[4]{0:T(128)} %eps_in.1, f32[2,3,8,32,128]{4,3,2,1,0:T(8,128)} %e_in.1, ...), custom_call_target="tpu_custom_call" | custom-call | tf_op jit(solution)/shard_map/pallas_call | solution.py:394
  22.7 1.2 %shard_map.77 = (f32[2,3,8,32,128]{4,3,2,1,0:T(8,128)}, f32[2,3,8,32,128]{4,3,2,1,0:T(8,128)}, f32[8,32,128]{2,1,0:T(8,128)}) custom-call(f32[2,3,8,32,128]{4,3,2,1,0:T(8,128)S(1)} %get-tuple-element.9.e_in, f32[8,32,128]{2,1,0:T(8,128)S(1)} %get-tuple-element.10.g_in, f32[2,3,8,32,128]{4,3,2,1,0:T(8,128)S(1)} %get-tuple-element.11.h_in, ...), custom_call_target="tpu_custom_call" | custom-call | tf_op jit(solution)/shard_map/pallas_call | solution.py:432

commit v4 on v3

--- a/solution.py
+++ b/solution.py
@@ -69,7 +69,7 @@
     ("xmyp", (-1, 1, 0)), ("zmyp", (0, 1, -1)), ("zmxp", (1, 0, -1)),
 )
 FIRST = (
-    ("ey0", (0, -1, 0)), ("ey2", (0, -1, 0)), ("em", (0, -1, 0)), ("ex", (-1, 0, 0)), ("ez", (0, 0, -1)),
+    ("em", (0, -1, 0)), ("ex", (-1, 0, 0)), ("ez", (0, 0, -1)),
 )
 SENDS = FACES + EDGES + FIRST
 
@@ -78,7 +78,7 @@
            eps, fwd, mat, inv, kx, ky, kz,
            xp, xp_s, xm_s, ed, zp, zm, xp_r, xm_r, yp_r, ym_r, zp_r, zm_r,
            ymzp_r, ymxp_r, xmzp_r, xmyp_r, zmyp_r, zmxp_r,
-           ex, ez, ex_r, ey_r, em_r, ez_r, load_sem, send_sem, recv_sem):
+           ex, ez, ex_r, ys, em_r, ez_r, load_sem, send_sem, recv_sem):
     steps = fwd.shape[0]
     ny, nz, nx = mat.shape
     axes = ("gx", "gy", "gz")
@@ -116,7 +116,7 @@
             xm=(xm_s.at[n], xm_r.at[n]),
             yp0=(field.at[:, 0, ny - 1], yp_r.at[n, 0]),
             yp2=(field.at[:, 2, ny - 1], yp_r.at[n, 1]),
-            ym=(field.at[:, :, 0], ym_r.at[n]),
+            ym=(ys.at[n], ym_r.at[n]),
             zp=(zp.at[n], zp_r.at[n]),
             zm=(zm.at[n], zm_r.at[n]),
             ymzp=(ed.at[n], ymzp_r.at[n]),
@@ -128,8 +128,6 @@
         )
         if n == 0:
             ends.update(
-                ey0=(e_in.at[:, 0, 0], ey_r.at[0]),
-                ey2=(e_in.at[:, 2, 0], ey_r.at[1]),
                 em=(mat_in.at[0], em_r),
                 ex=(ex, ex_r),
                 ez=(ez, ez_r),
@@ -281,15 +279,22 @@
 
     def front_y(n):
         scale = time_step * ky[...]
-        ahead = [rot(ym_r[n, 0, c], ym_r[n, 1, c], y_ahead) for c in range(3)]
+        part_x = rot(ym_r[n, 0, 0], ym_r[n, 0, 1], y_ahead)
+        part_z = rot(ym_r[n, 1, 0], ym_r[n, 1, 1], y_ahead)
         below = rot(ymzp_r[n, 0:1, :], ymzp_r[n, 1:2, :], y_ahead)
         corner = rot_packed(rot_packed(unfold(ymxp_r[n])[0], y_ahead), x_behind)
         for s in range(2):
-            hx, hy, hz = (ahead[c][s] for c in range(3))
-            hy_z = shift(hy, jnp.where(z_first, 0.0, below[s]), 0)
-            hy_x = shift(hy, corner[:, s * ny:s * ny + 1], 1)
-            ry[0, s] = ry[0, s] - scale * ((hz - h[s, 2, ny - 1]) - (hy - hy_z))
-            ry[1, s] = ry[1, s] - scale * ((hy - hy_x) - (hx - h[s, 0, ny - 1]))
+            hy_z = jnp.where(row == 0, jnp.where(z_first, 0.0, below[s]), 0.0)
+            hy_x = jnp.where(lane == 0, corner[:, s * ny:s * ny + 1], 0.0)
+            ry[0, s] = part_x[s] + scale * (h[s, 2, ny - 1] - hy_z)
+            ry[1, s] = part_z[s] + scale * (hy_x - h[s, 0, ny - 1])
+
+    def send_part(n):
+        scale = time_step * inv[0]
+        for s in range(2):
+            hx, hy, hz = (h[s, c, 0] for c in range(3))
+            ys[n, 0, s] = e[s, 0, 0] - scale * (hz - (hy - shift(hy, 0.0, 0)))
+            ys[n, 1, s] = e[s, 2, 0] - scale * ((hy - shift(hy, 0.0, 1)) - hx)
 
     def gradient(n):
         for y in range(ny):
@@ -302,7 +307,7 @@
             g[y] = total if n == 0 else g[y] + total
 
     now = copies(0)
-    start(now, "yp0", "yp2", "ym", "em", "ey0", "ey2")
+    start(now, "yp0", "yp2", "em")
     load_h.wait()
     packed = [blank] * 5
     for y in range(ny):
@@ -323,6 +328,8 @@
     for y in range(ny):
         inv[y] = inverse(mat[y])
     load_e.wait()
+    send_part(0)
+    now["ym"].start()
     packed = [blank] * 3
     for y in range(ny):
         for s in range(2):
@@ -348,11 +355,10 @@
                 load_fwd.wait()
             gradient(n)
         if n == 0:
-            landed(now, "ex", "ez", "em", "ey0", "ey2")
+            landed(now, "ex", "ez", "em")
             ex_u = unfold(ex_r[0])
             for i in range(2):
                 px[i] = rot_packed(ex_u[i], x_ahead)
-                ry[i, 0], ry[i, 1] = rot(ey_r[i, 0], ey_r[i, 1], y_ahead)
                 for c in range(2):
                     rz[i, c] = ez_r[2 * i + c]
             kx[...] = unfold(ex_r[1])[0]
@@ -373,6 +379,7 @@
             update_h(y)
             packed = pack(packed, n + 1, y)
             if y == 0:
+                send_part(n + 1)
                 later["ym"].start()
             if y == ny - 1:
                 start(later, "yp0", "yp2")
@@ -413,12 +420,12 @@
             pltpu.VMEM((ny, nx), f32),
             *(pltpu.VMEM((steps, *shape), f32) for shape in (
                 (2, nz, nx), (8, nx), (2, 8, nx), (8, nx), (2, 2, ny, nx), (2, 3, ny, nx),
-                (8, nx), (2, 8, nx), (2, 2, nz, nx), (2, 3, nz, nx),
+                (8, nx), (2, 8, nx), (2, 2, nz, nx), (2, 2, nz, nx),
                 (2, 2, ny, nx), (2, 3, ny, nx), *[(8, nx)] * 6)),
             pltpu.VMEM((2, 8, nx), f32),
             pltpu.VMEM((5, ny, nx), f32),
             pltpu.VMEM((2, 8, nx), f32),
-            pltpu.VMEM((2, 2, nz, nx), f32),
+            pltpu.VMEM((steps, 2, 2, nz, nx), f32),
             pltpu.VMEM((nz, nx), material.dtype),
             pltpu.VMEM((5, ny, nx), f32),
             pltpu.SemaphoreType.DMA((5,)),

time: 24.1 us -> 20.9 us (0.87)
  Pallas kernels: 23.3 us -> 20.1 us
    pallas_call x1, Pallas kernels: 22 us -> 18.9 us  [shards(): pl.pallas_call(functools.partial(kernel, counts), out_shape=(pltpu.VMEM(a...]
where the time goes in v4:
time: 20.9 us; the launch traced here: 20.7 us
  Pallas kernels  20.1 us (96%)
  between operations  0.64 us (3%)
    pallas_call x1, Pallas kernels, shards(): pl.pallas_call(functools.partial(kernel, counts), out_shape=(pltpu.VMEM(a...  18.9 us
    pallas_call x1, Pallas kernels, shards(): pl.pallas_call(finish, out_shape=(jax.ShapeDtypeStruct(adj_e.shape, f32),...  1.22 us

profile of v4, /device:TPU:0, one launch (start us, length us, event | category | flops | bytes accessed | tf_op | source)
XLA Modules:
  0.0 20.7 jit_solution(14895013684827262449)
XLA Ops:
  0.6 18.9 %shard_map.76 = (f32[2,3,8,32,128]{4,3,2,1,0:T(8,128)S(1)}, f32[2,3,8,32,128]{4,3,2,1,0:T(8,128)S(1)}, f32[8,32,128]{2,1,0:T(8,128)S(1)}, f32[2,32,128]{2,1,0:T(...) custom-call(f32[4]{0:T(128)} %eps_in.1, f32[2,3,8,32,128]{4,3,2,1,0:T(8,128)} %e_in.1, ...), custom_call_target="tpu_custom_call" | custom-call | tf_op jit(solution)/shard_map/pallas_call | solution.py:401
  19.5 1.2 %shard_map.77 = (f32[2,3,8,32,128]{4,3,2,1,0:T(8,128)}, f32[2,3,8,32,128]{4,3,2,1,0:T(8,128)}, f32[8,32,128]{2,1,0:T(8,128)}) custom-call(f32[2,3,8,32,128]{4,3,2,1,0:T(8,128)S(1)} %get-tuple-element.9.e_in, f32[8,32,128]{2,1,0:T(8,128)S(1)} %get-tuple-element.10.g_in, f32[2,3,8,32,128]{4,3,2,1,0:T(8,128)S(1)} %get-tuple-element.11.h_in, ...), custom_call_target="tpu_custom_call" | custom-call | tf_op jit(solution)/shard_map/pallas_call | solution.py:439
